TPU v7x, 256 devices: a whole 4x4x8 slice. The times are simulated.
256 devices in a mesh: section: 2 (over x_lo), dp: 16 (over z, x_hi), feat: 8 (over y, core).
Axes of the slice: x: 4 (x_hi: 2, x_lo: 2; x = x_hi * 2 + x_lo), y: 4, z: 8, core: 2. Of those that a mesh axis runs over, the one named last changes fastest.
Arguments:
- context: bfloat16 [2048, 4096], P(None, ('section', 'feat')), may hold values from -6 to 6
- w_out: bfloat16 [4096, 4608], P(('section', 'feat'), 'dp')
- residual: bfloat16 [2048, 4608], P(None, 'dp'), may hold values from -6 to 6
- norm_gain: float32 [4608], P('dp'), may hold values from 0.5 to 1.5
- w_enc: bfloat16 [4608, 65536], P('dp', ('section', 'feat')), may hold values from -0.09375 to 0.09375
- b_enc: float32 [65536], P(('section', 'feat')), may hold values from -1 to 1
- w_dec: bfloat16 [65536, 4608], P(('section', 'feat'), 'dp'), may hold values from -0.125 to 0.125
- b_dec: float32 [4608], P('dp'), may hold values from -3 to 3
- block_slots: int32 [16, 16, 2], P(None, ('section', 'feat')), may hold values from -1 to 511, as said below
Outputs:
- grad_enc: bfloat16 [4608, 65536], P('dp', ('section', 'feat'))
- grad_dec: bfloat16 [65536, 4608], P(('section', 'feat'), 'dp')
Inputs may be any that keep to these rules, and one draw needn't show every extreme that they name: `block_slots`: entry [t, s, :] lists distinct blocks of shard s, that is ids s * 32 to (s + 1) * 32 - 1, live ones first and -1 after them; every tile has 16 live slots in all, and some shard with all 2 slots live.
All inputs are finite; a program needn't handle non-finite values.
Results may differ from a plain program's by a relative error of at most 0.04.
Values may be sent and summed in bfloat16 or wider, within the bound.
A program may use at most 128 MiB of HBM per device.

v0:
```python
import jax
import jax.numpy as jnp
from jax import lax
from jax.sharding import PartitionSpec as P

BLOCK = 128
SLOTS = 2
TILE = 128


norm_eps = 1e-06


def group_total(partial_term):
    return lax.psum(partial_term.astype(jnp.bfloat16), ("section", "feat")).astype(jnp.float32)


def tile_spread(table, first_tile, tile_span):
    picked = lax.dynamic_slice_in_dim(table, first_tile, tile_span, 0)
    expanded = jnp.broadcast_to(picked[:, None], (tile_span, TILE) + picked.shape[1:])
    return expanded.reshape(tile_span * TILE, -1)


def silu_slope(pre_act):
    sigmoid_pre = jax.nn.sigmoid(pre_act)
    return sigmoid_pre * (1.0 + pre_act * (1.0 - sigmoid_pre))


def body(context, w_out, residual, norm_gain, w_enc, b_enc, w_dec, b_dec, block_slots):
    token_total = context.shape[0]
    local_width = residual.shape[1]
    full_width = local_width * lax.axis_size("dp")
    share_size = token_total // lax.axis_size("dp")
    share_tiles = share_size // TILE
    tile_count = token_total // TILE
    block_count = w_enc.shape[1] // BLOCK
    slot_width = SLOTS * BLOCK
    first_tile = lax.axis_index("dp") * share_tiles
    attention = group_total(jnp.dot(context, w_out, preferred_element_type=jnp.float32))
    row_power = lax.psum(jnp.sum(attention * attention, axis=1), "dp")
    inv_rms = lax.rsqrt(row_power / full_width + norm_eps)
    stream = (
        residual.astype(jnp.float32) + attention * inv_rms[:, None] * norm_gain[None, :]
    ).astype(jnp.bfloat16)
    block_ids = block_slots.reshape(tile_count, SLOTS)
    live_mask = block_ids >= 0
    safe_ids = jnp.where(live_mask, block_ids % block_count, 0)
    live_table = jnp.broadcast_to(
        live_mask.astype(jnp.float32)[:, :, None], (tile_count, SLOTS, BLOCK)
    )
    bias_table = jnp.take(b_enc.reshape(block_count, BLOCK), safe_ids, axis=0)
    enc_blocks = jnp.take(w_enc.reshape(local_width, block_count, BLOCK), safe_ids, axis=1)
    dec_blocks = jnp.take(w_dec.reshape(block_count, BLOCK, local_width), safe_ids, axis=0)
    stream_tiles = stream.reshape(tile_count, TILE, local_width)
    mask_mine = tile_spread(live_table, first_tile, share_tiles)
    token_rows = stream_tiles
    weights = enc_blocks
    product = jnp.einsum("tpd,dtsk->tpsk", token_rows, weights, preferred_element_type=jnp.float32)
    pre_all = lax.psum(product.reshape(token_total, slot_width).astype(jnp.bfloat16), "dp").astype(
        jnp.float32
    ) + tile_spread(bias_table, 0, tile_count)
    code_values = (jax.nn.silu(pre_all) * tile_spread(live_table, 0, tile_count)).astype(
        jnp.bfloat16
    )
    pre_mine = lax.dynamic_slice_in_dim(pre_all, first_tile * TILE, share_size, 0)
    code_tiles = code_values.reshape(tile_count, TILE, SLOTS, BLOCK)
    decoded = jnp.einsum(
        "tpsk,tskd->tpd", code_tiles, dec_blocks, preferred_element_type=jnp.float32
    )
    rebuilt = group_total(decoded.reshape(token_total, local_width))
    residual_error = rebuilt + b_dec[None, :] - stream.astype(jnp.float32)
    grad_out = (residual_error / TILE).astype(jnp.bfloat16)
    grad_tiles = grad_out.reshape(tile_count, TILE, local_width)
    flat_ids = safe_ids.reshape(tile_count * SLOTS)
    dec_terms = jnp.einsum(
        "tpsk,tpd->tskd", code_tiles, grad_tiles, preferred_element_type=jnp.float32
    )
    dec_terms = dec_terms.reshape(tile_count * SLOTS, BLOCK, local_width)
    grad_dec = jnp.zeros((block_count, BLOCK, local_width), jnp.float32).at[flat_ids].add(dec_terms)
    grad_dec = grad_dec.reshape(block_count * BLOCK, local_width).astype(jnp.bfloat16)
    token_rows = grad_tiles
    weights = dec_blocks
    product = jnp.einsum("tpd,tskd->tpsk", token_rows, weights, preferred_element_type=jnp.float32)
    back_mine = lax.psum_scatter(
        product.reshape(share_size * lax.axis_size("dp"), slot_width).astype(jnp.bfloat16),
        "dp",
        scatter_dimension=0,
        tiled=True,
    ).astype(jnp.float32)
    grad_pre = (back_mine * silu_slope(pre_mine) * mask_mine).astype(jnp.bfloat16)
    grad_pre_all = lax.all_gather(grad_pre, "dp", axis=0, tiled=True).reshape(
        tile_count, TILE, SLOTS, BLOCK
    )
    enc_terms = jnp.einsum(
        "tpd,tpsk->dtsk", stream_tiles, grad_pre_all, preferred_element_type=jnp.float32
    )
    enc_terms = enc_terms.reshape(local_width, tile_count * SLOTS, BLOCK)
    grad_enc = (
        jnp.zeros((local_width, block_count, BLOCK), jnp.float32).at[:, flat_ids].add(enc_terms)
    )
    grad_enc = grad_enc.reshape(local_width, block_count * BLOCK).astype(jnp.bfloat16)
    return (grad_enc, grad_dec)


def solution(mesh):
    placed = (
        P(None, ("section", "feat")),
        P(("section", "feat"), "dp"),
        P(None, "dp"),
        P("dp"),
        P("dp", ("section", "feat")),
        P(("section", "feat")),
        P(("section", "feat"), "dp"),
        P("dp"),
        P(None, ("section", "feat"), None),
    )
    return jax.shard_map(
        body,
        mesh=mesh,
        in_specs=placed,
        out_specs=(P("dp", ("section", "feat")), P(("section", "feat"), "dp")),
        check_vma=False,
    )
```

profile of v0, /device:TPU:4, one launch (start us, length us, event | category | flops | bytes accessed | tf_op | source)
XLA Modules:
  0.0 797.5 jit_solution(9702393983874569223)
XLA Ops:
  7.2 0.0 copy-start
  7.2 0.0 all-reduce.4.cloned.1.call-start
  7.2 2.9 convolution_convert_fusion
  10.2 0.0 all-reduce.4.cloned.1.call-update
  10.2 0.0 all-reduce.6.cloned.1.call-start
  10.2 0.6 compare_and_fusion
  10.8 0.7 copy.63
  11.5 0.1 copy.64
  11.6 0.1 reshape.244
  11.7 1.8 copy_bitcast_fusion.3
  13.5 4.0 gather_fusion
  17.5 121.0 %all-reduce.4.cloned.1.call-done = bf16[2048,288]{0,1:T(8,128)(2,1)} async-done(((bf16[2048,288]{0,1:T(8,128)(2,1)}), bf16[2048,288]{0,1:T(8,128)(2,1)}) %all-reduce.4.cloned.1.call-update) | async-done | bytes 1179664 | tf_op jit(solution)/shard_map/psum | solution.py:15
  138.6 1.5 fusion
  140.1 38.6 %psum.29 = f32[2048]{0:T(1024)S(1)} all-reduce(f32[2048]{0:T(1024)S(1)} %fusion), channel_id=1, replica_groups=mesh['section'=2,'dp'=16,'feat'=8] {'dp'}, use_global_device_ids=true, to_apply=%region_2.0 | all-reduce | flops 2048 | bytes 16384 | tf_op jit(solution)/shard_map/psum | solution.py:40
  178.8 0.0 copy-start.9
  178.8 2.0 fusion.39
  180.8 0.2 copy.104
  181.0 2.0 fusion.12
  183.1 1.9 copy.67
  185.0 1.2 copy.136
  186.3 0.0 all-reduce.6.cloned.1.call-update
  186.3 0.0 all-reduce.8.cloned.1.call-start
  186.4 0.6 gather_fusion.1
  186.9 0.1 broadcast_select_fusion.9
  187.0 0.8 copy.69
  187.8 2.1 copy_bitcast_fusion.2
  189.9 2.3 gather_fusion.2
  192.1 152.4 %all-reduce.6.cloned.1.call-done = bf16[2048,256]{0,1:T(8,128)(2,1)} async-done(((bf16[2048,256]{0,1:T(8,128)(2,1)}), bf16[2048,256]{0,1:T(8,128)(2,1)}) %all-reduce.6.cloned.1.call-update) | async-done | bytes 1048592 | tf_op jit(solution)/shard_map/psum | solution.py:59
  344.5 1.6 broadcast_in_dim.74
  346.1 0.9 broadcast_in_dim.75
  347.0 3.4 fusion.22
  350.4 1.2 copy.108
  351.6 2.4 copy.72
  354.0 2.0 fusion.15
  356.1 0.0 copy-start.14
  356.1 1.4 copy.134
  357.4 0.0 all-reduce.8.cloned.1.call-update
  357.5 0.2 reduce-scatter.4.cloned.1.call-start
  357.7 123.4 %all-reduce.8.cloned.1.call-done = bf16[2048,288]{0,1:T(8,128)(2,1)} async-done(((bf16[2048,288]{0,1:T(8,128)(2,1)}), bf16[2048,288]{0,1:T(8,128)(2,1)}) %all-reduce.8.cloned.1.call-update) | async-done | bytes 1179664 | tf_op jit(solution)/shard_map/psum | solution.py:15
  481.1 2.1 fusion.16
  483.2 0.2 copy.109
  483.5 1.4 copy-done.7
  484.9 1.1 fusion.11
  486.0 1.1 copy.97
  487.1 1.1 copy.135
  488.2 0.0 reduce-scatter.4.cloned.1.call-update
  488.2 0.0 all-gather.2.cloned.1.call-start
  488.3 0.2 dynamic-slice_reduce_fusion
  488.5 0.1 broadcast_bitcast_fusion
  488.5 202.8 %reduce-scatter.4.cloned.1.call-done = bf16[128,256]{1,0:T(8,128)(2,1)} async-done(((bf16[2048,256]{1,0:T(8,128)(2,1)}), bf16[128,256]{1,0:T(8,128)(2,1)}) %reduce-scatter.4.cloned.1.call-update) | async-done | bytes 65552
  691.4 0.9 copy.96
  692.3 1.6 multiply_convert_fusion.1
  694.0 0.0 all-gather.2.cloned.1.call-update
  694.0 0.1 copy.62
  694.1 0.1 reshape.228
  694.2 2.9 fusion.23
  697.1 2.8 broadcast_in_dim.81
  699.9 10.2 %scatter_fusion.1 = f32[32,128,288]{1,2,0:T(8,128)} fusion(f32[32,128,288]{1,2,0:T(8,128)} %broadcast_in_dim.81, s32[32]{0:T(128)S(1)} %fusion.35, f32[32,128,288]{1,2,0:T(8,128)} %bitcast.132), kind=kCustom, calls=%fused_computation.4 | custom fusion | flops 1179648 | bytes 14155904 | tf_op jit(solution)/shard_map/scatter-add | solution.py:79
  710.1 56.6 %all-gather.2.cloned.1.call-done = bf16[2048,256]{0,1:T(8,128)(2,1)} async-done(((bf16[128,256]{0,1:T(8,128)(2,1)}), bf16[2048,256]{0,1:T(8,128)(2,1)}) %all-gather.2.cloned.1.call-update) | async-done | bytes 1048592 | tf_op jit(solution)/shard_map/all_gather | solution.py:91
  766.8 1.4 copy.111
  768.2 3.0 fusion.20
  771.2 2.7 broadcast_in_dim.69
  773.9 10.2 %scatter_fusion = f32[288,32,128]{2,0,1:T(8,128)} fusion(f32[288,32,128]{2,0,1:T(8,128)} %broadcast_in_dim.69, s32[32]{0:T(128)S(1)} %fusion.35, f32[32,288,128]{2,1,0:T(8,128)} %bitcast.133), kind=kCustom, calls=%fused_computation.3 | custom fusion | flops 1179648 | bytes 14155904 | tf_op jit(solution)/shard_map/scatter-add | solution.py:99
  784.1 6.8 copy_bitcast_fusion
  (39 shorter events, 0.1 us)
Async XLA Ops:
  7.2 4.5 copy-start
  7.2 3.1 copy-start.12
  7.2 131.4 %all-reduce.4.cloned.1.call-start = ((), (), s32[]{:S(2)}) async-start(), calls=%async_computation.1 | async-start | bytes 2359296 | tf_op jit(solution)/shard_map/psum | solution.py:15
  10.2 334.3 %all-reduce.6.cloned.1.call-start = ((), (), s32[]{:S(2)}) async-start(), calls=%async_computation.2 | async-start | bytes 2097152 | tf_op jit(solution)/shard_map/psum | solution.py:59
  13.5 165.2 %copy-start.3 = (bf16[2048,288]{0,1:T(8,128)(2,1)S(1)}, bf16[2048,288]{0,1:T(8,128)(2,1)}, u32[]{:S(2)}) copy-start(bf16[2048,288]{0,1:T(8,128)(2,1)} %param.11) | copy-start | bytes 3538948
  13.5 165.2 %copy-start.13 = (f32[288]{0:T(512)S(1)}, f32[288]{0:T(512)}, u32[]{:S(2)}) copy-start(f32[288]{0:T(512)} %param.12) | copy-start | bytes 3460
  178.8 2.3 copy-start.9
  178.8 2.3 copy-start.15
  181.0 2.1 copy-start.4
  183.1 3.3 copy-start.10
  183.1 3.9 copy-start.16
  186.3 294.8 %all-reduce.8.cloned.1.call-start = ((), (), s32[]{:S(2)}) async-start(), calls=%async_computation.3 | async-start | bytes 2359296 | tf_op jit(solution)/shard_map/psum | solution.py:15
  344.5 2.5 copy-start.11
  350.4 3.6 copy-start.6
  350.4 3.6 copy-start.17
  356.1 125.1 %copy-start.2 = (bf16[2048,288]{0,1:T(8,128)(2,1)S(1)}, bf16[2048,288]{0,1:T(8,128)(2,1)}, u32[]{:S(2)}) copy-start(bf16[2048,288]{0,1:T(8,128)(2,1)} %all-reduce.4.cloned.1.call-done) | copy-start | bytes 3538948
  356.1 125.1 %copy-start.14 = (f32[288]{0:T(512)S(1)}, f32[288]{0:T(512)}, u32[]{:S(2)}) copy-start(f32[288]{0:T(512)} %param.12) | copy-start | bytes 3460
  357.5 333.9 %reduce-scatter.4.cloned.1.call-start = ((), (), s32[]{:S(2)}) async-start(), calls=%async_computation.5 | async-start | bytes 1114112
  481.1 2.4 copy-start.18
  483.2 1.7 copy-start.7
  486.0 208.2 %copy-start.8 = (bf16[16,128,2,128]{3,1,2,0:T(8,128)(2,1)S(1)}, bf16[16,128,2,128]{3,1,2,0:T(8,128)(2,1)}, u32[]{:S(2)}) copy-start(bf16[16,128,2,128]{3,1,2,0:T(8,128)(2,1)} %copy.72) | copy-start | bytes 3145732
  488.2 278.5 %all-gather.2.cloned.1.call-start = ((), (), s32[]{:S(2)}) async-start(), calls=%async_computation.4 | async-start | bytes 1114112 | tf_op jit(solution)/shard_map/all_gather | solution.py:91
  710.1 58.1 %copy-start.5 = (bf16[36,8,16,128]{3,2,1,0:T(8,128)(2,1)S(1)}, bf16[36,8,16,128]{3,2,1,0:T(8,128)(2,1)}, u32[]{:S(2)}) copy-start(bf16[36,8,16,128]{3,2,1,0:T(8,128)(2,1)} %copy-done.4) | copy-start | bytes 3538948
  784.1 6.8 copy-start.1
Sparse Core Ops, SparseCore 0:
  10.7 127.8 all-reduce.3
  186.4 158.0 all-reduce.5
  357.6 123.4 all-reduce.7
  488.3 202.9 reduce-scatter.3
  694.6 72.1 all-gather.1
where the time goes:
time: 800 us; the launch traced here: 797 us
  waiting for transfers between devices  656 us (82%)
  blocking collectives  38.6 us (5%)
  other arithmetic  38.5 us (5%)
  local copies, waits for them, and re-layouts  35.4 us (4%)
  between operations  14.1 us (2%)
  matrix products  14 us (2%)
    psum x2, waiting for transfers between devices, group_total(): lax.psum(partial_term.astype(jnp.bfloat16), ('section', 'feat'))  244 us
    unnamed x6, waiting for transfers between devices  203 us
    psum x1, waiting for transfers between devices, body(): lax.psum(product.reshape(token_total, slot_width).astype(jnp.bfloat16), '...  152 us
    all_gather x1, waiting for transfers between devices, body(): lax.all_gather(grad_pre, 'dp', axis=0, tiled=True)  56.6 us
    psum x1, blocking collectives, body(): row_power = lax.psum(jnp.sum(attention * attention, axis=1), 'dp')  38.6 us
  transfers between devices with their start and end apart: 5, of which 5 were waited for; matrix products, arithmetic and copies ran while one was open for 4% of the time, Pallas kernels for 0%

commit v1 on v0

v1 whole, which is shorter than its diff:
```python
import functools

import jax
import jax.numpy as jnp
from jax import lax
from jax.experimental import pallas as pl
from jax.experimental.pallas import tpu as pltpu
from jax.sharding import PartitionSpec as P

MESH = pl.DeviceIdType.MESH
BF16 = jnp.bfloat16
F32 = jnp.float32

BLOCK = 128
TILE = 128
SLOTS = 2
HALVES = 2
PART = 8
Z, Y = 8, 4
LAG = 1

norm_eps = 1e-06


def dot_nn(a, b):
    return lax.dot_general(a, b, (((1,), (0,)), ((), ())), preferred_element_type=F32)


def dot_nt(a, b):
    return lax.dot_general(a, b, (((1,), (1,)), ((), ())), preferred_element_type=F32)


class Place:
    def __init__(self):
        dp, feat = lax.axis_index("dp"), lax.axis_index("feat")
        self.xl = lax.axis_index("section")
        self.z, self.xh = dp // 2, dp % 2
        self.y, self.core = feat // 2, feat % 2

    def device(self, xl=None, z=None, xh=None, y=None, core=None):
        xl = self.xl if xl is None else xl
        z = self.z if z is None else z
        xh = self.xh if xh is None else xh
        y = self.y if y is None else y
        core = self.core if core is None else core
        return (xl, z * 2 + xh, y * 2 + core)

    def sibling(self):
        return self.device(core=1 - self.core)

    def x_partner(self):
        return self.device(xh=1 - self.xh)

    def group_chip(self, code, sign):
        xl = (self.xl + code // Y) % 2
        y = (self.y + sign * (code % Y) + Y) % Y
        return xl, y

    def group_device(self, code):
        xl, y = self.group_chip(code, 1)
        return self.device(xl=xl, y=y)

    def z_device(self, step):
        return self.device(z=(self.z + step) % Z)

    def dp_device(self, code):
        return self.device(z=(self.z + code // 2) % Z, xh=(self.xh + code % 2) % 2)


def exchange_kernel(
    blocks_ref,
    live_ref,
    ctx_ref,
    w_out_ref,
    gain_ref,
    b_enc_ref,
    b_dec_ref,
    resid_hbm,
    w_enc_hbm,
    w_dec_hbm,
    stream_out,
    gp_out,
    codes_out,
    go_out,
    w_enc,
    w_dec,
    resid,
    enc_t,
    dec_t,
    cols,
    a_part,
    a_core,
    a_sum,
    a_in,
    d_part,
    d_core,
    d_sum,
    d_in,
    c_part,
    c_x,
    c_sum,
    c_in,
    e_part,
    e_x,
    e_sum,
    e_in,
    stream,
    go,
    codes,
    gp,
    power,
    power_core,
    power_in,
    local_sem,
    block_sem,
    out_sem,
    s_sem,
    r_sem,
):
    at = Place()
    me = at
    full_width = w_out_ref.shape[0] * lax.axis_size("dp")
    half_rows = w_out_ref.shape[0] // 2

    barrier = pltpu.get_barrier_semaphore()
    friends = [at.sibling()]
    friends += [at.group_device(code) for code in range(1, 8)]
    friends += [at.dp_device(code) for code in range(1, 16)]
    for friend in friends:
        pl.semaphore_signal(barrier, inc=1, device_id=friend, device_id_type=MESH)

    def block_load(src, dst, number, block):
        lanes = pl.ds(pl.multiple_of(block * BLOCK, BLOCK), BLOCK)
        return pltpu.make_async_copy(
            src.at[:, lanes], dst.at[block], block_sem.at[number, block]
        )

    def start_blocks(src, dst, number):
        def one(block, carry):
            block_load(src, dst, number, block).start()
            return carry

        lax.fori_loop(0, dst.shape[0], one, 0)

    def wait_blocks(src, dst, number):
        def one(block, carry):
            block_load(src, dst, number, block).wait()
            return carry

        lax.fori_loop(0, dst.shape[0], one, 0)

    resid_load = pltpu.make_async_copy(resid_hbm, resid, local_sem.at[0])
    resid_load.start()
    start_blocks(w_enc_hbm, w_enc, 0)
    start_blocks(w_dec_hbm, w_dec, 1)

    count = [0]
    sent = []

    def send(src, dst, device):
        slot = count[0]
        count[0] += 1
        copy = pltpu.make_async_remote_copy(
            src_ref=src,
            dst_ref=dst,
            send_sem=s_sem.at[slot],
            recv_sem=r_sem.at[slot],
            device_id=device,
            device_id_type=MESH,
        )
        copy.start()
        sent.append(copy)
        return copy

    def columns_of(ref, tile, slot):
        return ref[blocks_ref[tile, slot]]

    def rows_of(value):
        return value.reshape(2, half_rows, TILE)


    def group_reduce(h, product, part, core_in, total, arrived):
        copies = []
        for quarter in range(2):
            tiles = pl.ds(quarter * 4, 4)

            def one(j, carry, quarter=quarter):
                tile = quarter * 4 + j
                value = rows_of(product(tile).astype(BF16))
                part[h, 0, tile] = value[0]
                part[h, 1, tile] = value[1]
                return carry

            lax.fori_loop(0, 4, one, 0)
            if h == 0 and quarter == 0 and part is a_part:
                pl.semaphore_wait(barrier, len(friends))
            copies.append(
                send(part.at[h, 1 - me.core, tiles], core_in.at[h, tiles], at.sibling())
            )
        yield
        for copy in copies:
            copy.wait_recv()
        copies = []
        for code in range(1, 8):
            xl, y = at.group_chip(code, 1)
            j = xl * Y + y
            total[h, j] = (
                part[h, me.core, j].astype(F32) + core_in[h, j].astype(F32)
            ).astype(BF16)
            copies.append(
                send(total.at[h, j], arrived.at[h, code - 1], at.group_device(code))
            )
        j = me.xl * Y + me.y
        own = part[h, me.core, j].astype(F32) + core_in[h, j].astype(F32)
        yield
        for code in range(1, 8):
            copies[code - 1].wait_recv()
            own += arrived[h, code - 1].astype(F32)
        return own

    def group_gather(h, value, table):
        mine = me.xl * Y + me.y
        table[h, mine, me.core] = value
        copies = []
        for code in range(1, 8):
            region = table.at[h, mine, me.core]
            copies.append(send(region, region, at.group_device(code)))
        region = table.at[h, mine, me.core]
        forwards = [send(region, region, at.sibling())]
        yield
        for code in range(1, 8):
            copies[code - 1].wait_recv()
            xl, y = at.group_chip(code, -1)
            region = table.at[h, xl * Y + y, me.core]
            forwards.append(send(region, region, at.sibling()))
        yield
        for copy in forwards:
            copy.wait_recv()

    def dp_reduce(h, product, part, x_in, total, arrived):
        copies = []
        for quarter in range(2):
            tiles = pl.ds(quarter * 4, 4)

            def one(j, carry, quarter=quarter):
                tile = quarter * 4 + j
                first, second = product(tile)
                part[h, 0, tile] = first.astype(BF16)
                part[h, 1, tile] = second.astype(BF16)
                return carry

            lax.fori_loop(0, 4, one, 0)
            copies.append(
                send(part.at[h, 1 - me.xh, tiles], x_in.at[h, tiles], at.x_partner())
            )
        yield
        for copy in copies:
            copy.wait_recv()
        copies = []
        for step in range(1, 8):
            j = (me.z + step) % Z
            total[h, j] = (
                part[h, me.xh, j].astype(F32) + x_in[h, j].astype(F32)
            ).astype(BF16)
            copies.append(send(total.at[h, j], arrived.at[h, step - 1], at.z_device(step)))
        own = part[h, me.xh, me.z].astype(F32) + x_in[h, me.z].astype(F32)
        yield
        for step in range(1, 8):
            copies[step - 1].wait_recv()
            own += arrived[h, step - 1].astype(F32)
        return own

    def dp_gather(h, value, table):
        table[h, me.z, me.xh] = value
        region = table.at[h, me.z, me.xh]
        copies = [send(region, region, at.z_device(step)) for step in range(1, 8)]
        forwards = [send(region, region, at.x_partner())]
        yield
        for step in range(1, 8):
            copies[step - 1].wait_recv()
            region = table.at[h, (me.z - step + Z) % Z, me.xh]
            forwards.append(send(region, region, at.x_partner()))
        yield
        for copy in forwards:
            copy.wait_recv()

    outs = []

    def write_out(h, table, out, number):
        copy = pltpu.make_async_copy(
            table.at[h], out.at[h], out_sem.at[h * 4 + number]
        )
        copy.start()
        outs.append(copy)

    def half(h):
        def attention(tile):
            rows = ctx_ref[pl.ds(pl.multiple_of((h * PART + tile) * TILE, TILE), TILE), :]
            return dot_nt(w_out_ref[...], rows)

        attn = yield from group_reduce(h, attention, a_part, a_core, a_sum, a_in)
        power[h] = jnp.sum(attn * attn, axis=0, keepdims=True)
        copy = send(power.at[h], power_core.at[h], at.sibling())
        yield
        copy.wait_recv()
        power_in[h, 0] = power[h] + power_core[h]
        copies = [
            send(power_in.at[h, 0], power_in.at[h, code], at.dp_device(code))
            for code in range(1, 16)
        ]
        yield
        for copy in copies:
            copy.wait_recv()
        row_power = power_in[h, 0]
        for code in range(1, 16):
            row_power += power_in[h, code]
        inv_rms = lax.rsqrt(row_power / full_width + norm_eps)
        rows = pl.ds(pl.multiple_of(me.core * half_rows, 16), half_rows)
        if h == 0:
            resid_load.wait()
        tile = h * PART + me.xl * Y + me.y
        lanes = pl.ds(pl.multiple_of(tile * TILE, TILE), TILE)
        value = resid[rows, lanes].astype(F32) + attn * inv_rms * cols[0, rows, :]
        mine = value.astype(BF16)
        yield from group_gather(h, mine, stream)
        write_out(h, stream, stream_out, 0)

        def encode(tile):
            pair = dot_nn(enc_t[h * PART + tile], stream[h, tile].reshape(2 * half_rows, TILE))
            return pair[:BLOCK], pair[BLOCK:]

        pre = yield from dp_reduce(h, encode, c_part, c_x, c_sum, c_in)
        own_tile = h * PART + me.z
        alive = live_ref[pl.ds(own_tile * SLOTS + me.xh, 1), :]
        bias = b_enc_ref[blocks_ref[own_tile, me.xh]]
        bias = jnp.broadcast_to(bias, (BLOCK, TILE))
        pre = pre + bias.T
        sigmoid = 1.0 / (1.0 + jnp.exp(-pre))
        code_values = (pre * sigmoid * alive).astype(BF16)
        slope = sigmoid * (1.0 + pre * (1.0 - sigmoid)) * alive
        yield from dp_gather(h, code_values, codes)
        write_out(h, codes, codes_out, 1)

        def decode(tile):
            pair = codes[h, tile]
            return dot_nn(columns_of(w_dec, h * PART + tile, 0), pair[0]) + dot_nn(
                columns_of(w_dec, h * PART + tile, 1), pair[1]
            )

        rebuilt = yield from group_reduce(h, decode, d_part, d_core, d_sum, d_in)
        grad_out = (rebuilt + cols[1, rows, :] - mine.astype(F32)) / TILE
        yield from group_gather(h, grad_out.astype(BF16), go)
        write_out(h, go, go_out, 2)

        def backward(tile):
            pair = dot_nn(dec_t[h * PART + tile], go[h, tile].reshape(2 * half_rows, TILE))
            return pair[:BLOCK], pair[BLOCK:]

        back = yield from dp_reduce(h, backward, e_part, e_x, e_sum, e_in)
        yield from dp_gather(h, (back * slope).astype(BF16), gp)
        write_out(h, gp, gp_out, 3)

    def turned_blocks(table, out):
        def one(tile, carry):
            out[tile, 0:BLOCK, :] = columns_of(table, tile, 0).T
            out[tile, BLOCK : 2 * BLOCK, :] = columns_of(table, tile, 1).T
            return carry

        lax.fori_loop(0, HALVES * PART, one, 0)

    def prepare(step):
        if step == 0:
            for number, ref in enumerate((gain_ref, b_dec_ref)):
                cols[number] = jnp.broadcast_to(ref[...], (TILE, ref.shape[1])).T
            wait_blocks(w_enc_hbm, w_enc, 0)
            turned_blocks(w_enc, enc_t)
        if step == 6:
            wait_blocks(w_dec_hbm, w_dec, 1)
            turned_blocks(w_dec, dec_t)

    runs = [half(h) for h in range(HALVES)]
    running = [True] * HALVES
    step = 0
    while any(running):
        for h in range(HALVES):
            if running[h] and step >= h * LAG:
                try:
                    next(runs[h])
                except StopIteration:
                    running[h] = False
        prepare(step)
        step += 1
    for copy in sent:
        copy.wait_send()
    for copy in outs:
        copy.wait()


SENDS = 2 * (2 * (9 + 15 + 2 - 2) + 2 * (2 + 7 + 15) + 16)


def exchange(blocks, live, ctx, w_out_t, gain, b_enc, b_dec, resid_t, w_enc, w_dec_t):
    width = w_out_t.shape[0]
    half_rows = width // 2
    blocks_here = w_enc.shape[1] // BLOCK
    tiles = HALVES * PART
    vmem = pl.BlockSpec(memory_space=pltpu.VMEM)
    hbm = pl.BlockSpec(memory_space=pl.ANY)
    wide = (HALVES, PART, 2, half_rows, TILE)
    narrow = (HALVES, PART, SLOTS, BLOCK, TILE)
    group_sets = [
        pltpu.VMEM((HALVES, 2, PART, half_rows, TILE), BF16),
        pltpu.VMEM((HALVES, PART, half_rows, TILE), BF16),
        pltpu.VMEM((HALVES, PART, half_rows, TILE), BF16),
        pltpu.VMEM((HALVES, 7, half_rows, TILE), BF16),
    ]
    dp_sets = [
        pltpu.VMEM((HALVES, SLOTS, PART, BLOCK, TILE), BF16),
        pltpu.VMEM((HALVES, PART, BLOCK, TILE), BF16),
        pltpu.VMEM((HALVES, PART, BLOCK, TILE), BF16),
        pltpu.VMEM((HALVES, 7, BLOCK, TILE), BF16),
    ]
    scratch = [
        pltpu.VMEM((blocks_here, width, BLOCK), BF16),
        pltpu.VMEM((blocks_here, width, BLOCK), BF16),
        pltpu.VMEM(resid_t.shape, BF16),
        pltpu.VMEM((tiles, SLOTS * BLOCK, width), BF16),
        pltpu.VMEM((tiles, SLOTS * BLOCK, width), BF16),
        pltpu.VMEM((2, width, TILE), F32),
        *group_sets,
        *group_sets,
        *dp_sets,
        *dp_sets,
        pltpu.VMEM(wide, BF16),
        pltpu.VMEM(wide, BF16),
        pltpu.VMEM(narrow, BF16),
        pltpu.VMEM(narrow, BF16),
        pltpu.VMEM((HALVES, 1, TILE), F32),
        pltpu.VMEM((HALVES, 1, TILE), F32),
        pltpu.VMEM((HALVES, 16, 1, TILE), F32),
        pltpu.SemaphoreType.DMA((1,)),
        pltpu.SemaphoreType.DMA((2, blocks_here)),
        pltpu.SemaphoreType.DMA((HALVES * 4,)),
        pltpu.SemaphoreType.DMA((SENDS,)),
        pltpu.SemaphoreType.DMA((SENDS,)),
    ]
    return pl.pallas_call(
        exchange_kernel,
        out_shape=(
            jax.ShapeDtypeStruct(wide, BF16),
            jax.ShapeDtypeStruct(narrow, BF16),
            jax.ShapeDtypeStruct(narrow, BF16),
            jax.ShapeDtypeStruct(wide, BF16),
        ),
        in_specs=[pl.BlockSpec(memory_space=pltpu.SMEM)] + [vmem] * 6 + [hbm] * 3,
        out_specs=(hbm,) * 4,
        scratch_shapes=scratch,
        compiler_params=pltpu.CompilerParams(
            collective_id=0, has_side_effects=True, vmem_limit_bytes=52 << 20
        ),
    )(blocks, live, ctx, w_out_t, gain, b_enc, b_dec, resid_t, w_enc, w_dec_t)


def gradient_kernel(
    blocks_ref, stream, gp, codes, go, enc_out, dec_out, enc_sum, dec_sum
):
    enc_sum[...] = jnp.zeros_like(enc_sum)
    dec_sum[...] = jnp.zeros_like(dec_sum)
    width = enc_sum.shape[0]

    def one(tile, carry):
        h, j = tile // PART, tile % PART
        rows = stream[h, j].reshape(width, TILE)
        errors = go[h, j].reshape(width, TILE)
        enc = dot_nt(rows, gp[h, j].reshape(SLOTS * BLOCK, TILE))
        dec = dot_nt(errors, codes[h, j].reshape(SLOTS * BLOCK, TILE))
        for slot in range(SLOTS):
            block = blocks_ref[tile, slot]
            lanes = pl.ds(pl.multiple_of(block * BLOCK, BLOCK), BLOCK)
            mine = slice(slot * BLOCK, (slot + 1) * BLOCK)
            enc_sum[:, lanes] += enc[:, mine]
            dec_sum[:, lanes] += dec[:, mine]
        return carry

    lax.fori_loop(0, HALVES * PART, one, 0)
    enc_out[...] = enc_sum[...].astype(BF16)
    dec_out[...] = dec_sum[...].astype(BF16)


def gradients(blocks, stream, gp, codes, go, shape):
    vmem = pl.BlockSpec(memory_space=pltpu.VMEM)
    return pl.pallas_call(
        gradient_kernel,
        out_shape=(jax.ShapeDtypeStruct(shape, BF16),) * 2,
        in_specs=[pl.BlockSpec(memory_space=pltpu.SMEM)] + [vmem] * 4,
        out_specs=(vmem,) * 2,
        scratch_shapes=[pltpu.VMEM(shape, F32)] * 2,
        compiler_params=pltpu.CompilerParams(vmem_limit_bytes=48 << 20),
    )(blocks, stream, gp, codes, go)


def body(context, w_out, residual, norm_gain, w_enc, b_enc, w_dec, b_dec, block_slots):
    ids = block_slots.reshape(-1, SLOTS)
    alive = ids >= 0
    blocks = jnp.where(alive, ids % (w_enc.shape[1] // BLOCK), 0)
    live = jnp.broadcast_to(alive.reshape(-1, 1), (alive.size, TILE)).astype(F32)
    stream, gp, codes, go = exchange(
        blocks,
        live,
        context,
        w_out.T,
        norm_gain.reshape(1, -1),
        b_enc.reshape(-1, 1, BLOCK),
        b_dec.reshape(1, -1),
        residual.T,
        w_enc,
        w_dec.T,
    )
    grad_enc, grad_dec_t = gradients(blocks, stream, gp, codes, go, w_enc.shape)
    return grad_enc, grad_dec_t.T


def solution(mesh):
    placed = (
        P(None, ("section", "feat")),
        P(("section", "feat"), "dp"),
        P(None, "dp"),
        P("dp"),
        P("dp", ("section", "feat")),
        P(("section", "feat")),
        P(("section", "feat"), "dp"),
        P("dp"),
        P(None, ("section", "feat"), None),
    )
    return jax.shard_map(
        body,
        mesh=mesh,
        in_specs=placed,
        out_specs=(P("dp", ("section", "feat")), P(("section", "feat"), "dp")),
        check_vma=False,
    )
```

time: 800 us -> 157 us (0.20)
  waiting for transfers between devices: 656 us -> 0 us
  Pallas kernels: 0 us -> 147 us
  blocking collectives: 38.6 us -> 0 us
  other arithmetic: 38.5 us -> 0.7 us
  local copies, waits for them, and re-layouts: 35.4 us -> 7.75 us
  matrix products: 14 us -> 0 us
  between operations: 14.1 us -> 0.66 us
    psum x3 -> x0, waiting for transfers between devices: 397 us -> none  [the longest x2 244 us: group_total(): lax.psum(partial_term.astype(jnp.bfloat16), ('section', 'feat'))]
    unnamed x6 -> x0, waiting for transfers between devices: 203 us -> none
    pallas_call x0 -> x2, Pallas kernels: none -> 147 us  [the longest x1 139 us: exchange(): pl.pallas_call(exchange_kernel, out_shape=(jax.ShapeDtypeStruct(wide, BF1...]
    all_gather x1 -> x0, waiting for transfers between devices: 56.6 us -> none  [body(): lax.all_gather(grad_pre, 'dp', axis=0, tiled=True)]
    psum x1 -> x0, blocking collectives: 38.6 us -> none  [body(): row_power = lax.psum(jnp.sum(attention * attention, axis=1), 'dp')]
    scatter-add x2 -> x0, other arithmetic: 20.4 us -> none  [the longest x1 10.2 us: body(): jnp.zeros((block_count, BLOCK, local_width), jnp.float32).at[flat_ids]]
    dot_general x6 -> x0, matrix products: 14 us -> none  [the longest x1 2.98 us: body(): jnp.einsum('tpd,tpsk->dtsk', stream_tiles, grad_pre_all, preferred_elemen...]
  transfers between devices with their start and end apart: 5 -> 0, of which waited for: 5 -> 0; matrix products, arithmetic and copies ran while one was open for 4% -> 0% of each run, Pallas kernels for 0% -> 0%
where the time goes in v1:
time: 157 us; the launch traced here: 156 us
  Pallas kernels  147 us (94%)
  local copies, waits for them, and re-layouts  7.75 us (5%)
    pallas_call x1, Pallas kernels, exchange(): pl.pallas_call(exchange_kernel, out_shape=(jax.ShapeDtypeStruct(wide, BF1...  139 us
    pallas_call x1, Pallas kernels, gradients(): pl.pallas_call(gradient_kernel, out_shape=(jax.ShapeDtypeStruct(shape, BF...  8.72 us
    unnamed x10, local copies, waits for them, and re-layouts  5.39 us

profile of v1, /device:TPU:4, one launch (start us, length us, event | category | flops | bytes accessed | tf_op | source)
XLA Modules:
  0.0 156.5 jit_solution(124933865587279345)
XLA Ops:
  0.6 0.7 compare_convert_fusion
  1.3 0.7 reshape.27.gain_ref
  2.0 0.7 reshape.29.b_dec_ref
  2.7 0.1 copy.20
  2.8 0.1 reshape.30
  2.9 0.8 copy.16
  3.6 0.1 broadcast_in_dim.4.live_ref
  3.7 0.0 copy-start.3
  3.7 0.9 copy-done.3
  4.6 0.0 copy-start.4
  4.6 0.7 copy-done.4
  5.3 138.7 %shard_map.104 = (bf16[2,8,2,144,128]{4,3,2,1,0:T(8,128)(2,1)}, bf16[2,8,2,128,128]{4,3,2,1,0:T(8,128)(2,1)S(1)}, bf16[2,8,2,128,128]{4,3,2,1,0:T(8,128)(2,1)}, bf16[2,8,2,144,128]{4,3,2,1,0:T(8,128)(2,1)}) custom-call(s32[16,2]{1,0:T(8,128)S(1)} %fusion.1.blocks_ref, f32[32,128]{1,0:T(8,128)S(1)} %broadcast_in_dim.4.live_ref, bf16[2048,256]{1,0:T(8,128)(2,1)} %ctx_ref.1, ...), custom_call_target="tpu_custom_call" | custom-call | tf_op jit(solution)/shard_map/pallas_call | solution.py:447
  144.0 0.0 copy-start
  144.0 1.3 copy-done
  145.3 0.0 copy-start.1
  145.3 1.3 copy-done.1
  146.5 0.0 copy-start.2
  146.5 1.2 copy-done.2
  147.8 8.7 %shard_map.105 = (bf16[288,4096]{1,0:T(8,128)(2,1)}, bf16[288,4096]{1,0:T(8,128)(2,1)}) custom-call(s32[16,2]{1,0:T(8,128)S(1)} %fusion.1.blocks_ref, bf16[2,8,2,144,128]{4,3,2,1,0:T(8,128)(2,1)S(1)} %copy-done, bf16[2,8,2,128,128]{4,3,2,1,0:T(8,128)(2,1)S(1)} %get-tuple-element.9.gp, bf16[2,8,2,128,128]{4,3,2,1,0:T(8,128)(2,1)S(1)} %copy-done.2, ...), custom_call_target="tpu_custom_call" | custom-call | tf_op jit(solution)/shard_map/pallas_call | solution.py:492
  (1 shorter events, 0.0 us)
Async XLA Ops:
  3.7 0.9 copy-start.3
  4.6 0.7 copy-start.4
  144.0 1.3 copy-start
  145.3 1.3 copy-start.1
  146.5 1.2 copy-start.2

commit v2 on v1

v2 whole, which is shorter than its diff:
```python
import functools

import jax
import jax.numpy as jnp
from jax import lax
from jax.experimental import pallas as pl
from jax.experimental.pallas import tpu as pltpu
from jax.sharding import PartitionSpec as P

MESH = pl.DeviceIdType.MESH
BF16 = jnp.bfloat16
F32 = jnp.float32

BLOCK = 128
TILE = 128
SLOTS = 2
HALVES = 2
PART = 8
Z, Y = 8, 4
GROUP_ORDER = (6, 5, 7, 2, 4, 1, 3, 0)
GROUP_NEAR = (1, 3, 4, 2, 5, 7, 6)
Z_ORDER = (4, 3, 5, 2, 6, 1, 7, 0)
Z_NEAR = (1, 7, 2, 6, 3, 5, 4)
EARLY = 4
CHUNK = 2
CHORE_TIME, STEP_TIME = 0.5, 0.7

norm_eps = 1e-06


def dot_nn(a, b):
    return lax.dot_general(a, b, (((1,), (0,)), ((), ())), preferred_element_type=F32)


def dot_nt(a, b):
    return lax.dot_general(a, b, (((1,), (1,)), ((), ())), preferred_element_type=F32)


class Place:
    def __init__(self):
        dp, feat = lax.axis_index("dp"), lax.axis_index("feat")
        self.xl = lax.axis_index("section")
        self.z, self.xh = dp // 2, dp % 2
        self.y, self.core = feat // 2, feat % 2

    def device(self, xl=None, z=None, xh=None, y=None, core=None):
        xl = self.xl if xl is None else xl
        z = self.z if z is None else z
        xh = self.xh if xh is None else xh
        y = self.y if y is None else y
        core = self.core if core is None else core
        return (xl, z * 2 + xh, y * 2 + core)

    def sibling(self):
        return self.device(core=1 - self.core)

    def x_partner(self):
        return self.device(xh=1 - self.xh)

    def group_chip(self, code, sign):
        xl = (self.xl + code // Y) % 2
        y = (self.y + sign * (code % Y) + Y) % Y
        return xl, y

    def group_device(self, code):
        xl, y = self.group_chip(code, 1)
        return self.device(xl=xl, y=y)

    def z_device(self, step):
        return self.device(z=(self.z + step) % Z)

    def dp_device(self, code):
        return self.device(z=(self.z + code // 2) % Z, xh=(self.xh + code % 2) % 2)


def exchange_kernel(
    blocks_ref,
    live_ref,
    rows_ref,
    b_enc_ref,
    ctx_hbm,
    w_out_hbm,
    resid_hbm,
    w_enc_hbm,
    w_dec_hbm,
    stream_out,
    gp_out,
    codes_out,
    go_out,
    ctx_ref,
    w_out_ref,
    w_enc,
    w_dec,
    resid,
    enc_t,
    dec_t,
    cols,
    a_part,
    a_core,
    a_sum,
    a_in,
    d_part,
    d_core,
    d_sum,
    d_in,
    c_part,
    c_x,
    c_sum,
    c_in,
    e_part,
    e_x,
    e_sum,
    e_in,
    stream,
    go,
    codes,
    gp,
    power,
    power_core,
    power_in,
    local_sem,
    block_sem,
    out_sem,
    s_sem,
    r_sem,
):
    at = Place()
    me = at
    full_width = w_out_ref.shape[0] * lax.axis_size("dp")
    half_rows = w_out_ref.shape[0] // 2

    barrier = pltpu.get_barrier_semaphore()
    friends = [at.sibling()]
    friends += [at.group_device(code) for code in range(1, 8)]
    friends += [at.dp_device(code) for code in range(1, 16)]
    for friend in friends:
        pl.semaphore_signal(barrier, inc=1, device_id=friend, device_id_type=MESH)

    def block_load(src, dst, number, block):
        lanes = pl.ds(pl.multiple_of(block * BLOCK, BLOCK), BLOCK)
        return pltpu.make_async_copy(
            src.at[:, lanes], dst.at[block], block_sem.at[number, block]
        )

    def start_blocks(src, dst, number):
        def one(block, carry):
            block_load(src, dst, number, block).start()
            return carry

        lax.fori_loop(0, dst.shape[0], one, 0)

    def wait_blocks(src, dst, number):
        def one(block, carry):
            block_load(src, dst, number, block).wait()
            return carry

        lax.fori_loop(0, dst.shape[0], one, 0)

    loads = [
        pltpu.make_async_copy(src, dst, local_sem.at[number])
        for number, (src, dst) in enumerate(
            ((ctx_hbm, ctx_ref), (w_out_hbm, w_out_ref), (resid_hbm, resid))
        )
    ]
    for load in loads:
        load.start()
    start_blocks(w_enc_hbm, w_enc, 0)
    start_blocks(w_dec_hbm, w_dec, 1)

    count = [0]
    sent = []

    def send(src, dst, device):
        slot = count[0]
        count[0] += 1
        copy = pltpu.make_async_remote_copy(
            src_ref=src,
            dst_ref=dst,
            send_sem=s_sem.at[slot],
            recv_sem=r_sem.at[slot],
            device_id=device,
            device_id_type=MESH,
        )
        copy.start()
        sent.append(copy)
        return copy

    def columns_of(ref, tile, slot):
        return ref[blocks_ref[slot, tile]]

    def rows_of(value):
        return value.reshape(2, half_rows, TILE)


    def group_part(h, spot, product, part):
        xl, y = at.group_chip(GROUP_ORDER[spot], 1)
        value = rows_of(product(xl * Y + y).astype(BF16))
        part[h, 0, spot] = value[0]
        part[h, 1, spot] = value[1]

    def group_reduce(h, product, part, core_in, total, arrived):
        copies = []
        for first in range(0, PART, 2):
            spots = pl.ds(first, 2)
            if product is not None:
                group_part(h, first, product, part)
                group_part(h, first + 1, product, part)
            copies.append(
                send(part.at[h, 1 - me.core, spots], core_in.at[h, spots], at.sibling())
            )
        yield 1.5
        copies_on = []
        for spot, code in enumerate(GROUP_ORDER):
            if spot % 2 == 0:
                copies[spot // 2].wait_recv()
            value = part[h, me.core, spot].astype(F32) + core_in[h, spot].astype(F32)
            if code == 0:
                own = value
                continue
            total[h, spot] = value.astype(BF16)
            copies_on.append(
                send(total.at[h, spot], arrived.at[h, code - 1], at.group_device(code))
            )
        yield 5.0
        for copy, code in zip(copies_on, GROUP_ORDER):
            copy.wait_recv()
            own += arrived[h, code - 1].astype(F32)
        return own

    def group_gather(h, value, table):
        mine = me.xl * Y + me.y
        table[h, mine, me.core] = value
        region = table.at[h, mine, me.core]
        copies = [send(region, region, at.group_device(code)) for code in GROUP_NEAR]
        forwards = [send(region, region, at.sibling())]
        yield 5.0
        for copy, code in zip(copies, GROUP_NEAR):
            copy.wait_recv()
            xl, y = at.group_chip(code, -1)
            region = table.at[h, xl * Y + y, me.core]
            forwards.append(send(region, region, at.sibling()))
        yield 1.5
        for copy in forwards:
            copy.wait_recv()

    def dp_reduce(h, product, part, x_in, total, arrived):
        copies = []
        for first in range(0, PART, 2):
            for spot in (first, first + 1):
                pair = product((me.z + Z_ORDER[spot]) % Z).astype(BF16)
                part[h, 0, spot] = pair[:BLOCK]
                part[h, 1, spot] = pair[BLOCK:]
            spots = pl.ds(first, 2)
            copies.append(
                send(part.at[h, 1 - me.xh, spots], x_in.at[h, spots], at.x_partner())
            )
        yield 4.0
        copies_on = []
        for spot, step in enumerate(Z_ORDER):
            if spot % 2 == 0:
                copies[spot // 2].wait_recv()
            value = part[h, me.xh, spot].astype(F32) + x_in[h, spot].astype(F32)
            if step == 0:
                own = value
                continue
            total[h, spot] = value.astype(BF16)
            copies_on.append(
                send(total.at[h, spot], arrived.at[h, step - 1], at.z_device(step))
            )
        yield 6.0
        for copy, step in zip(copies_on, Z_ORDER):
            copy.wait_recv()
            own += arrived[h, step - 1].astype(F32)
        return own

    def dp_gather(h, value, table):
        table[h, me.z, me.xh] = value
        region = table.at[h, me.z, me.xh]
        copies = [send(region, region, at.z_device(step)) for step in Z_NEAR]
        forwards = [send(region, region, at.x_partner())]
        yield 6.0
        for copy, step in zip(copies, Z_NEAR):
            copy.wait_recv()
            region = table.at[h, (me.z - step + Z) % Z, me.xh]
            forwards.append(send(region, region, at.x_partner()))
        yield 3.0
        for copy in forwards:
            copy.wait_recv()

    outs = []

    def write_out(h, table, out, number):
        copy = pltpu.make_async_copy(
            table.at[h], out.at[h], out_sem.at[h * 4 + number]
        )
        copy.start()
        outs.append(copy)

    def half(h):
        attn = yield from group_reduce(h, None, a_part, a_core, a_sum, a_in)
        power[h] = jnp.sum(attn * attn, axis=0, keepdims=True)
        copy = send(power.at[h], power_core.at[h], at.sibling())
        yield 1.5
        copy.wait_recv()
        power_in[h, 0] = power[h] + power_core[h]
        copies = [
            send(power_in.at[h, 0], power_in.at[h, code], at.dp_device(code))
            for code in range(1, 16)
        ]
        yield 4.5
        for copy in copies:
            copy.wait_recv()
        row_power = power_in[h, 0]
        for code in range(1, 16):
            row_power += power_in[h, code]
        inv_rms = lax.rsqrt(row_power / full_width + norm_eps)
        rows = pl.ds(pl.multiple_of(me.core * half_rows, 16), half_rows)
        if h == 0:
            loads[2].wait()
        tile = h * PART + me.xl * Y + me.y
        lanes = pl.ds(pl.multiple_of(tile * TILE, TILE), TILE)
        value = resid[rows, lanes].astype(F32) + attn * inv_rms * cols[0, rows, :]
        mine = value.astype(BF16)
        yield from group_gather(h, mine, stream)
        write_out(h, stream, stream_out, 0)

        ensure(0, h)

        def encode(tile):
            rows = stream[h, tile].reshape(2 * half_rows, TILE)
            return dot_nn(enc_t[h * PART + tile], rows)

        pre = yield from dp_reduce(h, encode, c_part, c_x, c_sum, c_in)
        own_tile = h * PART + me.z
        alive = live_ref[me.xh, pl.ds(own_tile, 1), :]
        bias = b_enc_ref[blocks_ref[me.xh, own_tile]]
        bias = jnp.broadcast_to(bias, (BLOCK, TILE))
        pre = pre + bias.T
        sigmoid = 1.0 / (1.0 + jnp.exp(-pre))
        code_values = (pre * sigmoid * alive).astype(BF16)
        slope = sigmoid * (1.0 + pre * (1.0 - sigmoid)) * alive
        yield from dp_gather(h, code_values, codes)
        write_out(h, codes, codes_out, 1)

        if 1 not in waited:
            waited.add(1)
            wait_blocks(w_dec_hbm, w_dec, 1)

        def decode(tile):
            pair = codes[h, tile]
            return dot_nn(columns_of(w_dec, h * PART + tile, 0), pair[0]) + dot_nn(
                columns_of(w_dec, h * PART + tile, 1), pair[1]
            )

        rebuilt = yield from group_reduce(h, decode, d_part, d_core, d_sum, d_in)
        grad_out = (rebuilt + cols[1, rows, :] - mine.astype(F32)) / TILE
        yield from group_gather(h, grad_out.astype(BF16), go)
        write_out(h, go, go_out, 2)

        ensure(1, h)

        def backward(tile):
            rows = go[h, tile].reshape(2 * half_rows, TILE)
            return dot_nn(dec_t[h * PART + tile], rows)

        back = yield from dp_reduce(h, backward, e_part, e_x, e_sum, e_in)
        yield from dp_gather(h, (back * slope).astype(BF16), gp)
        write_out(h, gp, gp_out, 3)

    def turn(table, out, first):
        def one(tile, carry):
            out[tile, 0:BLOCK, :] = columns_of(table, tile, 0).T
            out[tile, BLOCK : 2 * BLOCK, :] = columns_of(table, tile, 1).T
            return carry

        lax.fori_loop(first, first + CHUNK, one, 0)

    waited = set()
    chores = [
        (number, first)
        for number in range(2)
        for first in range(0, HALVES * PART, CHUNK)
    ]

    def chore():
        number, first = chores.pop(0)
        src, table, out = (
            (w_enc_hbm, w_enc, enc_t),
            (w_dec_hbm, w_dec, dec_t),
        )[number]
        if number not in waited:
            waited.add(number)
            wait_blocks(src, table, number)
        turn(table, out, first)

    def ensure(number, h):
        while chores and chores[0] < (number, (h + 1) * PART):
            chore()

    loads[0].wait()
    loads[1].wait()
    for h in range(HALVES):

        def attention(tile, h=h):
            rows = ctx_ref[pl.ds(pl.multiple_of((h * PART + tile) * TILE, TILE), TILE), :]
            return dot_nt(w_out_ref[...], rows)

        for spot in range(PART):
            group_part(h, spot, attention, a_part)
    for number in range(2):
        row = rows_ref[pl.ds(number, 1), :]
        cols[number] = jnp.broadcast_to(row, (TILE, row.shape[1])).T
    for _ in range(EARLY):
        chore()
    pl.semaphore_wait(barrier, len(friends))
    runs = [half(h) for h in range(HALVES)]
    due = [float(h) for h in range(HALVES)]
    clock = 0.0
    started = False
    while runs:
        h = min(range(len(runs)), key=lambda i: due[i])
        while chores and clock + CHORE_TIME < due[h] and started:
            chore()
            clock += CHORE_TIME
        clock = max(clock, due[h]) + STEP_TIME
        try:
            due[h] = clock + next(runs[h])
        except StopIteration:
            del runs[h], due[h]
        started = True
    for copy in sent:
        copy.wait_send()
    for copy in outs:
        copy.wait()


SENDS = HALVES * (4 * (4 + 7 + 15) + 16)


def exchange(blocks, live, ctx, w_out_t, gain_bias, b_enc, resid_t, w_enc, w_dec_t):
    width = w_out_t.shape[0]
    half_rows = width // 2
    blocks_here = w_enc.shape[1] // BLOCK
    tiles = HALVES * PART
    vmem = pl.BlockSpec(memory_space=pltpu.VMEM)
    hbm = pl.BlockSpec(memory_space=pl.ANY)
    wide = (HALVES, PART, 2, half_rows, TILE)
    narrow = (HALVES, PART, SLOTS, BLOCK, TILE)
    group_sets = [
        pltpu.VMEM((HALVES, 2, PART, half_rows, TILE), BF16),
        pltpu.VMEM((HALVES, PART, half_rows, TILE), BF16),
        pltpu.VMEM((HALVES, PART, half_rows, TILE), BF16),
        pltpu.VMEM((HALVES, 7, half_rows, TILE), BF16),
    ]
    dp_sets = [
        pltpu.VMEM((HALVES, SLOTS, PART, BLOCK, TILE), BF16),
        pltpu.VMEM((HALVES, PART, BLOCK, TILE), BF16),
        pltpu.VMEM((HALVES, PART, BLOCK, TILE), BF16),
        pltpu.VMEM((HALVES, 7, BLOCK, TILE), BF16),
    ]
    scratch = [
        pltpu.VMEM(ctx.shape, BF16),
        pltpu.VMEM(w_out_t.shape, BF16),
        pltpu.VMEM((blocks_here, width, BLOCK), BF16),
        pltpu.VMEM((blocks_here, width, BLOCK), BF16),
        pltpu.VMEM(resid_t.shape, BF16),
        pltpu.VMEM((tiles, SLOTS * BLOCK, width), BF16),
        pltpu.VMEM((tiles, SLOTS * BLOCK, width), BF16),
        pltpu.VMEM((2, width, TILE), F32),
        *group_sets,
        *group_sets,
        *dp_sets,
        *dp_sets,
        pltpu.VMEM(wide, BF16),
        pltpu.VMEM(wide, BF16),
        pltpu.VMEM(narrow, BF16),
        pltpu.VMEM(narrow, BF16),
        pltpu.VMEM((HALVES, 1, TILE), F32),
        pltpu.VMEM((HALVES, 1, TILE), F32),
        pltpu.VMEM((HALVES, 16, 1, TILE), F32),
        pltpu.SemaphoreType.DMA((3,)),
        pltpu.SemaphoreType.DMA((2, blocks_here)),
        pltpu.SemaphoreType.DMA((HALVES * 4,)),
        pltpu.SemaphoreType.DMA((SENDS,)),
        pltpu.SemaphoreType.DMA((SENDS,)),
    ]
    return pl.pallas_call(
        exchange_kernel,
        out_shape=(
            jax.ShapeDtypeStruct(wide, BF16),
            jax.ShapeDtypeStruct(narrow, BF16),
            jax.ShapeDtypeStruct(narrow, BF16),
            jax.ShapeDtypeStruct(wide, BF16),
        ),
        in_specs=[pl.BlockSpec(memory_space=pltpu.SMEM)] + [vmem] * 3 + [hbm] * 5,
        out_specs=(hbm,) * 4,
        scratch_shapes=scratch,
        compiler_params=pltpu.CompilerParams(
            collective_id=0, has_side_effects=True, vmem_limit_bytes=52 << 20
        ),
    )(blocks, live, gain_bias, b_enc, ctx, w_out_t, resid_t, w_enc, w_dec_t)


def gradient_kernel(
    blocks_ref,
    stream_hbm,
    gp_hbm,
    codes_hbm,
    go_hbm,
    enc_out,
    dec_out,
    stream,
    gp,
    codes,
    go,
    total,
    result,
    in_sem,
    out_sem,
):
    loads = [
        pltpu.make_async_copy(src, dst, in_sem.at[number])
        for number, (src, dst) in enumerate(
            ((codes_hbm, codes), (go_hbm, go), (stream_hbm, stream), (gp_hbm, gp))
        )
    ]
    for load in loads:
        load.start()
    total[...] = jnp.zeros_like(total)
    width, features = total.shape[1:]
    share = features // 4
    writes = []
    for number, (left, right, out) in enumerate(
        ((go, codes, dec_out), (stream, gp, enc_out))
    ):
        loads[2 * number].wait()
        loads[2 * number + 1].wait()

        def one(tile, carry, number=number, left=left, right=right):
            h, j = tile // PART, tile % PART
            terms = dot_nt(
                left[h, j].reshape(width, TILE), right[h, j].reshape(SLOTS * BLOCK, TILE)
            )
            for slot in range(SLOTS):
                block = blocks_ref[slot, tile]
                lanes = pl.ds(pl.multiple_of(block * BLOCK, BLOCK), BLOCK)
                total[number, :, lanes] += terms[:, slot * BLOCK : (slot + 1) * BLOCK]
            return carry

        lax.fori_loop(0, HALVES * PART, one, 0, unroll=4)
        for quarter in range(4):
            lanes = pl.ds(quarter * share, share)
            result[number, :, lanes] = total[number, :, lanes].astype(BF16)
            write = pltpu.make_async_copy(
                result.at[number, :, lanes], out.at[:, lanes], out_sem.at[number, quarter]
            )
            write.start()
            writes.append(write)
    for write in writes:
        write.wait()


def gradients(blocks, stream, gp, codes, go, shape):
    hbm = pl.BlockSpec(memory_space=pl.ANY)
    return pl.pallas_call(
        gradient_kernel,
        out_shape=(jax.ShapeDtypeStruct(shape, BF16),) * 2,
        in_specs=[pl.BlockSpec(memory_space=pltpu.SMEM)] + [hbm] * 4,
        out_specs=(hbm,) * 2,
        scratch_shapes=[
            pltpu.VMEM(stream.shape, BF16),
            pltpu.VMEM(gp.shape, BF16),
            pltpu.VMEM(codes.shape, BF16),
            pltpu.VMEM(go.shape, BF16),
            pltpu.VMEM((2, *shape), F32),
            pltpu.VMEM((2, *shape), BF16),
            pltpu.SemaphoreType.DMA((4,)),
            pltpu.SemaphoreType.DMA((2, 4)),
        ],
        compiler_params=pltpu.CompilerParams(vmem_limit_bytes=52 << 20),
    )(blocks, stream, gp, codes, go)


def body(context, w_out, residual, norm_gain, w_enc, b_enc, w_dec, b_dec, block_slots):
    ids = block_slots[:, 0, :].T
    alive = ids >= 0
    blocks = jnp.where(alive, ids % (w_enc.shape[1] // BLOCK), 0)
    live = jnp.broadcast_to(alive[:, :, None], (*alive.shape, TILE)).astype(F32)
    stream, gp, codes, go = exchange(
        blocks,
        live,
        context,
        w_out.T,
        jnp.stack([norm_gain, b_dec]),
        b_enc.reshape(-1, 1, BLOCK),
        residual.T,
        w_enc,
        w_dec.T,
    )
    grad_enc, grad_dec_t = gradients(blocks, stream, gp, codes, go, w_enc.shape)
    return grad_enc, grad_dec_t.T


def solution(mesh):
    placed = (
        P(None, ("section", "feat")),
        P(("section", "feat"), "dp"),
        P(None, "dp"),
        P("dp"),
        P("dp", ("section", "feat")),
        P(("section", "feat")),
        P(("section", "feat"), "dp"),
        P("dp"),
        P(None, ("section", "feat"), None),
    )
    return jax.shard_map(
        body,
        mesh=mesh,
        in_specs=placed,
        out_specs=(P("dp", ("section", "feat")), P(("section", "feat"), "dp")),
        check_vma=False,
    )
```

time: 157 us -> 139 us (0.89); the launches traced: 156 us -> 136 us
  Pallas kernels: 147 us -> 131 us
  local copies, waits for them, and re-layouts: 7.75 us -> 3.06 us
    pallas_call x1, Pallas kernels: 139 us -> 123 us  [exchange(): pl.pallas_call(exchange_kernel, out_shape=(jax.ShapeDtypeStruct(wide, BF1...]
    unnamed x10 -> x4, local copies, waits for them, and re-layouts: 5.39 us -> 1.63 us
    reshape x3 -> x0, local copies, waits for them, and re-layouts: 2.12 us -> none  [the longest x1 0.76 us: body(): ids = block_slots.reshape(-1, SLOTS)]
where the time goes in v2:
time: 139 us; the launch traced here: 136 us
  Pallas kernels  131 us (94%)
  local copies, waits for them, and re-layouts  3.06 us (2%)
    pallas_call x1, Pallas kernels, exchange(): pl.pallas_call(exchange_kernel, out_shape=(jax.ShapeDtypeStruct(wide, BF1...  123 us
    pallas_call x1, Pallas kernels, gradients(): pl.pallas_call(gradient_kernel, out_shape=(jax.ShapeDtypeStruct(shape, BF...  7.9 us

profile of v2, /device:TPU:4, one launch (start us, length us, event | category | flops | bytes accessed | tf_op | source)
XLA Modules:
  0.0 135.9 jit_solution(10956974216273843009)
XLA Ops:
  0.6 0.7 fusion.blocks_ref
  1.3 0.7 fusion.2
  2.0 0.7 stack.9
  2.7 0.7 stack.10
  3.4 0.1 broadcast_in_dim.4.live_ref
  3.4 0.0 copy-start
  3.5 0.9 copy-done
  4.4 0.0 copy-start.1
  4.4 0.7 copy-done.1
  5.1 122.9 %shard_map.104 = (bf16[2,8,2,144,128]{4,3,2,1,0:T(8,128)(2,1)}, bf16[2,8,2,128,128]{4,3,2,1,0:T(8,128)(2,1)S(1)}, bf16[2,8,2,128,128]{4,3,2,1,0:T(8,128)(2,1)}, bf16[2,8,2,144,128]{4,3,2,1,0:T(8,128)(2,1)}) custom-call(s32[2,16]{1,0:T(2,128)S(1)} %fusion.blocks_ref, f32[2,16,128]{2,1,0:T(8,128)S(1)} %broadcast_in_dim.4.live_ref, ...), custom_call_target="tpu_custom_call" | custom-call | tf_op jit(solution)/shard_map/pallas_call | solution.py:487
  128.0 7.9 %shard_map.105 = (bf16[288,4096]{1,0:T(8,128)(2,1)}, bf16[288,4096]{1,0:T(8,128)(2,1)}) custom-call(s32[2,16]{1,0:T(2,128)S(1)} %fusion.blocks_ref, bf16[2,8,2,144,128]{4,3,2,1,0:T(8,128)(2,1)} %get-tuple-element.8.stream_hbm, bf16[2,8,2,128,128]{4,3,2,1,0:T(8,128)(2,1)S(1)} %get-tuple-element.9.gp_hbm, ...), custom_call_target="tpu_custom_call" | custom-call | tf_op jit(solution)/shard_map/pallas_call | solution.py:565
  (1 shorter events, 0.0 us)
Async XLA Ops:
  3.4 0.9 copy-start
  4.4 0.7 copy-start.1

commit v3 on v2

--- a/solution.py
+++ b/solution.py
@@ -36,6 +36,10 @@
     return lax.dot_general(a, b, (((1,), (1,)), ((), ())), preferred_element_type=F32)
 
 
+def block_at(ids_ref, slot, tile, blocks):
+    return lax.rem(lax.max(ids_ref[slot, tile], 0), blocks)
+
+
 class Place:
     def __init__(self):
         dp, feat = lax.axis_index("dp"), lax.axis_index("feat")
@@ -74,10 +78,9 @@
 
 
 def exchange_kernel(
-    blocks_ref,
-    live_ref,
-    rows_ref,
-    b_enc_ref,
+    ids_ref,
+    rows_hbm,
+    b_enc_hbm,
     ctx_hbm,
     w_out_hbm,
     resid_hbm,
@@ -89,6 +92,8 @@
     go_out,
     ctx_ref,
     w_out_ref,
+    rows_ref,
+    b_enc_ref,
     w_enc,
     w_dec,
     resid,
@@ -159,7 +164,13 @@
     loads = [
         pltpu.make_async_copy(src, dst, local_sem.at[number])
         for number, (src, dst) in enumerate(
-            ((ctx_hbm, ctx_ref), (w_out_hbm, w_out_ref), (resid_hbm, resid))
+            (
+                (ctx_hbm, ctx_ref),
+                (w_out_hbm, w_out_ref),
+                (resid_hbm, resid),
+                (rows_hbm, rows_ref),
+                (b_enc_hbm, b_enc_ref),
+            )
         )
     ]
     for load in loads:
@@ -186,7 +197,7 @@
         return copy
 
     def columns_of(ref, tile, slot):
-        return ref[blocks_ref[slot, tile]]
+        return ref[block_at(ids_ref, slot, tile, ref.shape[0])]
 
     def rows_of(value):
         return value.reshape(2, half_rows, TILE)
@@ -315,8 +326,6 @@
             row_power += power_in[h, code]
         inv_rms = lax.rsqrt(row_power / full_width + norm_eps)
         rows = pl.ds(pl.multiple_of(me.core * half_rows, 16), half_rows)
-        if h == 0:
-            loads[2].wait()
         tile = h * PART + me.xl * Y + me.y
         lanes = pl.ds(pl.multiple_of(tile * TILE, TILE), TILE)
         value = resid[rows, lanes].astype(F32) + attn * inv_rms * cols[0, rows, :]
@@ -332,8 +341,8 @@
 
         pre = yield from dp_reduce(h, encode, c_part, c_x, c_sum, c_in)
         own_tile = h * PART + me.z
-        alive = live_ref[me.xh, pl.ds(own_tile, 1), :]
-        bias = b_enc_ref[blocks_ref[me.xh, own_tile]]
+        alive = lax.min(lax.max(ids_ref[me.xh, own_tile] + 1, 0), 1).astype(F32)
+        bias = b_enc_ref[block_at(ids_ref, me.xh, own_tile, b_enc_ref.shape[0])]
         bias = jnp.broadcast_to(bias, (BLOCK, TILE))
         pre = pre + bias.T
         sigmoid = 1.0 / (1.0 + jnp.exp(-pre))
@@ -397,8 +406,8 @@
         while chores and chores[0] < (number, (h + 1) * PART):
             chore()
 
-    loads[0].wait()
-    loads[1].wait()
+    for load in loads:
+        load.wait()
     for h in range(HALVES):
 
         def attention(tile, h=h):
@@ -437,12 +446,11 @@
 SENDS = HALVES * (4 * (4 + 7 + 15) + 16)
 
 
-def exchange(blocks, live, ctx, w_out_t, gain_bias, b_enc, resid_t, w_enc, w_dec_t):
+def exchange(ids, ctx, w_out_t, gain_bias, b_enc, resid_t, w_enc, w_dec_t):
     width = w_out_t.shape[0]
     half_rows = width // 2
     blocks_here = w_enc.shape[1] // BLOCK
     tiles = HALVES * PART
-    vmem = pl.BlockSpec(memory_space=pltpu.VMEM)
     hbm = pl.BlockSpec(memory_space=pl.ANY)
     wide = (HALVES, PART, 2, half_rows, TILE)
     narrow = (HALVES, PART, SLOTS, BLOCK, TILE)
@@ -461,6 +469,8 @@
     scratch = [
         pltpu.VMEM(ctx.shape, BF16),
         pltpu.VMEM(w_out_t.shape, BF16),
+        pltpu.VMEM(gain_bias.shape, F32),
+        pltpu.VMEM(b_enc.shape, F32),
         pltpu.VMEM((blocks_here, width, BLOCK), BF16),
         pltpu.VMEM((blocks_here, width, BLOCK), BF16),
         pltpu.VMEM(resid_t.shape, BF16),
@@ -478,7 +488,7 @@
         pltpu.VMEM((HALVES, 1, TILE), F32),
         pltpu.VMEM((HALVES, 1, TILE), F32),
         pltpu.VMEM((HALVES, 16, 1, TILE), F32),
-        pltpu.SemaphoreType.DMA((3,)),
+        pltpu.SemaphoreType.DMA((5,)),
         pltpu.SemaphoreType.DMA((2, blocks_here)),
         pltpu.SemaphoreType.DMA((HALVES * 4,)),
         pltpu.SemaphoreType.DMA((SENDS,)),
@@ -492,17 +502,17 @@
             jax.ShapeDtypeStruct(narrow, BF16),
             jax.ShapeDtypeStruct(wide, BF16),
         ),
-        in_specs=[pl.BlockSpec(memory_space=pltpu.SMEM)] + [vmem] * 3 + [hbm] * 5,
+        in_specs=[pl.BlockSpec(memory_space=pltpu.SMEM)] + [hbm] * 7,
         out_specs=(hbm,) * 4,
         scratch_shapes=scratch,
         compiler_params=pltpu.CompilerParams(
             collective_id=0, has_side_effects=True, vmem_limit_bytes=52 << 20
         ),
-    )(blocks, live, gain_bias, b_enc, ctx, w_out_t, resid_t, w_enc, w_dec_t)
+    )(ids, gain_bias, b_enc, ctx, w_out_t, resid_t, w_enc, w_dec_t)
 
 
 def gradient_kernel(
-    blocks_ref,
+    ids_ref,
     stream_hbm,
     gp_hbm,
     codes_hbm,
@@ -542,7 +552,7 @@
                 left[h, j].reshape(width, TILE), right[h, j].reshape(SLOTS * BLOCK, TILE)
             )
             for slot in range(SLOTS):
-                block = blocks_ref[slot, tile]
+                block = block_at(ids_ref, slot, tile, features // BLOCK)
                 lanes = pl.ds(pl.multiple_of(block * BLOCK, BLOCK), BLOCK)
                 total[number, :, lanes] += terms[:, slot * BLOCK : (slot + 1) * BLOCK]
             return carry
@@ -560,7 +570,7 @@
         write.wait()
 
 
-def gradients(blocks, stream, gp, codes, go, shape):
+def gradients(ids, stream, gp, codes, go, shape):
     hbm = pl.BlockSpec(memory_space=pl.ANY)
     return pl.pallas_call(
         gradient_kernel,
@@ -578,17 +588,13 @@
             pltpu.SemaphoreType.DMA((2, 4)),
         ],
         compiler_params=pltpu.CompilerParams(vmem_limit_bytes=52 << 20),
-    )(blocks, stream, gp, codes, go)
+    )(ids, stream, gp, codes, go)
 
 
 def body(context, w_out, residual, norm_gain, w_enc, b_enc, w_dec, b_dec, block_slots):
     ids = block_slots[:, 0, :].T
-    alive = ids >= 0
-    blocks = jnp.where(alive, ids % (w_enc.shape[1] // BLOCK), 0)
-    live = jnp.broadcast_to(alive[:, :, None], (*alive.shape, TILE)).astype(F32)
     stream, gp, codes, go = exchange(
-        blocks,
-        live,
+        ids,
         context,
         w_out.T,
         jnp.stack([norm_gain, b_dec]),
@@ -597,7 +603,7 @@
         w_enc,
         w_dec.T,
     )
-    grad_enc, grad_dec_t = gradients(blocks, stream, gp, codes, go, w_enc.shape)
+    grad_enc, grad_dec_t = gradients(ids, stream, gp, codes, go, w_enc.shape)
     return grad_enc, grad_dec_t.T
 
 

time: 139 us -> 137 us (0.986)
  no operation moved by 1% of the time
where the time goes in v3:
time: 137 us; the launch traced here: 135 us
  Pallas kernels  131 us (96%)
  local copies, waits for them, and re-layouts  3.67 us (3%)
    pallas_call x1, Pallas kernels, exchange(): pl.pallas_call(exchange_kernel, out_shape=(jax.ShapeDtypeStruct(wide, BF1...  123 us
    pallas_call x1, Pallas kernels, gradients(): pl.pallas_call(gradient_kernel, out_shape=(jax.ShapeDtypeStruct(shape, BF...  7.89 us

profile of v3, /device:TPU:4, one launch (start us, length us, event | category | flops | bytes accessed | tf_op | source)
XLA Modules:
  0.0 135.2 jit_solution(9027004077803546289)
XLA Ops:
  0.6 0.7 stack.9
  1.3 0.7 stack.10
  2.0 0.0 copy-start
  2.0 0.9 copy-done
  2.9 0.0 copy-start.1
  2.9 0.7 copy-done.1
  3.6 0.0 copy-start.2
  3.6 0.7 copy-done.2
  4.3 123.0 %shard_map.104 = (bf16[2,8,2,144,128]{4,3,2,1,0:T(8,128)(2,1)}, bf16[2,8,2,128,128]{4,3,2,1,0:T(8,128)(2,1)S(1)}, bf16[2,8,2,128,128]{4,3,2,1,0:T(8,128)(2,1)}, bf16[2,8,2,144,128]{4,3,2,1,0:T(8,128)(2,1)}) custom-call(s32[2,16]{1,0:T(2,128)S(1)} %bitcast.10, f32[2,288]{1,0:T(2,128)S(1)} %pad_maximum_fusion.rows_hbm, f32[32,1,128]{2,1,0:T(1,128)S(1)} %bitcast.9, ...), custom_call_target="tpu_custom_call" | custom-call | tf_op jit(solution)/shard_map/pallas_call | solution.py:497
  127.3 7.9 %shard_map.105 = (bf16[288,4096]{1,0:T(8,128)(2,1)}, bf16[288,4096]{1,0:T(8,128)(2,1)}) custom-call(s32[2,16]{1,0:T(2,128)S(1)} %bitcast.11, bf16[2,8,2,144,128]{4,3,2,1,0:T(8,128)(2,1)} %get-tuple-element.8.stream_hbm, bf16[2,8,2,128,128]{4,3,2,1,0:T(8,128)(2,1)S(1)} %get-tuple-element.9.gp_hbm, bf16[2,8,2,128,128]{4,3,2,1,0:T(8,128)(2,1)} %get-tuple-element.10.codes_hbm, ...), custom_call_target="tpu_custom_call" | custom-call | tf_op jit(solution)/shard_map/pallas_call | solution.py:575
  (1 shorter events, 0.0 us)
Async XLA Ops:
  2.0 0.9 copy-start
  2.9 0.7 copy-start.1
  3.6 0.7 copy-start.2

commit v4 on v3

--- a/solution.py
+++ b/solution.py
@@ -79,7 +79,8 @@
 
 def exchange_kernel(
     ids_ref,
-    rows_hbm,
+    gain_hbm,
+    b_dec_hbm,
     b_enc_hbm,
     ctx_hbm,
     w_out_hbm,
@@ -92,7 +93,8 @@
     go_out,
     ctx_ref,
     w_out_ref,
-    rows_ref,
+    gain_ref,
+    b_dec_ref,
     b_enc_ref,
     w_enc,
     w_dec,
@@ -168,7 +170,8 @@
                 (ctx_hbm, ctx_ref),
                 (w_out_hbm, w_out_ref),
                 (resid_hbm, resid),
-                (rows_hbm, rows_ref),
+                (gain_hbm, gain_ref),
+                (b_dec_hbm, b_dec_ref),
                 (b_enc_hbm, b_enc_ref),
             )
         )
@@ -416,8 +419,8 @@
 
         for spot in range(PART):
             group_part(h, spot, attention, a_part)
-    for number in range(2):
-        row = rows_ref[pl.ds(number, 1), :]
+    for number, ref in enumerate((gain_ref, b_dec_ref)):
+        row = ref[...].reshape(1, -1)
         cols[number] = jnp.broadcast_to(row, (TILE, row.shape[1])).T
     for _ in range(EARLY):
         chore()
@@ -446,12 +449,12 @@
 SENDS = HALVES * (4 * (4 + 7 + 15) + 16)
 
 
-def exchange(ids, ctx, w_out_t, gain_bias, b_enc, resid_t, w_enc, w_dec_t):
+def exchange(ids, ctx, w_out_t, gain, b_dec, b_enc, resid_t, w_enc, w_dec_t):
     width = w_out_t.shape[0]
     half_rows = width // 2
     blocks_here = w_enc.shape[1] // BLOCK
     tiles = HALVES * PART
-    hbm = pl.BlockSpec(memory_space=pl.ANY)
+    hbm = pl.BlockSpec(memory_space=pltpu.HBM)
     wide = (HALVES, PART, 2, half_rows, TILE)
     narrow = (HALVES, PART, SLOTS, BLOCK, TILE)
     group_sets = [
@@ -469,7 +472,8 @@
     scratch = [
         pltpu.VMEM(ctx.shape, BF16),
         pltpu.VMEM(w_out_t.shape, BF16),
-        pltpu.VMEM(gain_bias.shape, F32),
+        pltpu.VMEM(gain.shape, F32),
+        pltpu.VMEM(b_dec.shape, F32),
         pltpu.VMEM(b_enc.shape, F32),
         pltpu.VMEM((blocks_here, width, BLOCK), BF16),
         pltpu.VMEM((blocks_here, width, BLOCK), BF16),
@@ -488,7 +492,7 @@
         pltpu.VMEM((HALVES, 1, TILE), F32),
         pltpu.VMEM((HALVES, 1, TILE), F32),
         pltpu.VMEM((HALVES, 16, 1, TILE), F32),
-        pltpu.SemaphoreType.DMA((5,)),
+        pltpu.SemaphoreType.DMA((6,)),
         pltpu.SemaphoreType.DMA((2, blocks_here)),
         pltpu.SemaphoreType.DMA((HALVES * 4,)),
         pltpu.SemaphoreType.DMA((SENDS,)),
@@ -502,13 +506,13 @@
             jax.ShapeDtypeStruct(narrow, BF16),
             jax.ShapeDtypeStruct(wide, BF16),
         ),
-        in_specs=[pl.BlockSpec(memory_space=pltpu.SMEM)] + [hbm] * 7,
+        in_specs=[pl.BlockSpec(memory_space=pltpu.SMEM)] + [hbm] * 8,
         out_specs=(hbm,) * 4,
         scratch_shapes=scratch,
         compiler_params=pltpu.CompilerParams(
-            collective_id=0, has_side_effects=True, vmem_limit_bytes=52 << 20
+            collective_id=0, has_side_effects=True, vmem_limit_bytes=60 << 20
         ),
-    )(ids, gain_bias, b_enc, ctx, w_out_t, resid_t, w_enc, w_dec_t)
+    )(ids, gain, b_dec, b_enc, ctx, w_out_t, resid_t, w_enc, w_dec_t)
 
 
 def gradient_kernel(
@@ -571,7 +575,7 @@
 
 
 def gradients(ids, stream, gp, codes, go, shape):
-    hbm = pl.BlockSpec(memory_space=pl.ANY)
+    hbm = pl.BlockSpec(memory_space=pltpu.HBM)
     return pl.pallas_call(
         gradient_kernel,
         out_shape=(jax.ShapeDtypeStruct(shape, BF16),) * 2,
@@ -587,7 +591,7 @@
             pltpu.SemaphoreType.DMA((4,)),
             pltpu.SemaphoreType.DMA((2, 4)),
         ],
-        compiler_params=pltpu.CompilerParams(vmem_limit_bytes=52 << 20),
+        compiler_params=pltpu.CompilerParams(vmem_limit_bytes=60 << 20),
     )(ids, stream, gp, codes, go)
 
 
@@ -597,7 +601,8 @@
         ids,
         context,
         w_out.T,
-        jnp.stack([norm_gain, b_dec]),
+        norm_gain,
+        b_dec,
         b_enc.reshape(-1, 1, BLOCK),
         residual.T,
         w_enc,

time: 137 us -> 134 us (0.978)
  local copies, waits for them, and re-layouts: 3.67 us -> 0 us
    unnamed x6 -> x0, local copies, waits for them, and re-layouts: 2.3 us -> none
where the time goes in v4:
time: 134 us; the launch traced here: 132 us
  Pallas kernels  131 us (98%)
    pallas_call x1, Pallas kernels, exchange(): pl.pallas_call(exchange_kernel, out_shape=(jax.ShapeDtypeStruct(wide, BF1...  123 us
    pallas_call x1, Pallas kernels, gradients(): pl.pallas_call(gradient_kernel, out_shape=(jax.ShapeDtypeStruct(shape, BF...  8.04 us

profile of v4, /device:TPU:4, one launch (start us, length us, event | category | flops | bytes accessed | tf_op | source)
XLA Modules:
  0.0 132.1 jit_solution(8512102416923708597)
XLA Ops:
  0.6 123.5 %shard_map.104 = (bf16[2,8,2,144,128]{4,3,2,1,0:T(8,128)(2,1)}, bf16[2,8,2,128,128]{4,3,2,1,0:T(8,128)(2,1)}, bf16[2,8,2,128,128]{4,3,2,1,0:T(8,128)(2,1)}, bf16[2,8,2,144,128]{4,3,2,1,0:T(8,128)(2,1)}) custom-call(s32[2,16]{1,0:T(2,128)} %bitcast.12, f32[288]{0:T(512)} %gain_hbm.1, f32[288]{0:T(512)} %b_dec_hbm.1, f32[32,1,128]{2,1,0:T(1,128)} %bitcast.11, ...), custom_call_target="tpu_custom_call" | custom-call | tf_op jit(solution)/shard_map/pallas_call | solution.py:501
  124.1 8.0 %shard_map.105 = (bf16[288,4096]{1,0:T(8,128)(2,1)}, bf16[288,4096]{1,0:T(8,128)(2,1)}) custom-call(s32[2,16]{1,0:T(2,128)} %bitcast.13, bf16[2,8,2,144,128]{4,3,2,1,0:T(8,128)(2,1)} %get-tuple-element.8.stream_hbm, bf16[2,8,2,128,128]{4,3,2,1,0:T(8,128)(2,1)} %get-tuple-element.9.gp_hbm, bf16[2,8,2,128,128]{4,3,2,1,0:T(8,128)(2,1)} %get-tuple-element.10.codes_hbm, ...), custom_call_target="tpu_custom_call" | custom-call | tf_op jit(solution)/shard_map/pallas_call | solution.py:579
